TPU v7x, 128 devices: a whole 4x4x4 slice. The times are simulated.
128 devices in a mesh: row: 8 (over y, core), col: 4 (over x), layer: 4 (over z).
Axes of the slice: x: 4, y: 4, z: 4, core: 2. Of those that a mesh axis runs over, the one named last changes fastest.
Arguments:
- a_vals: bfloat16 [64, 16, 12, 128, 128], P('row', ('col', 'layer')), may hold values from -6 to 6
- a_cols: int32 [64, 16, 12], P('row', ('col', 'layer')), may hold values from 0 to 23, as said below
- b_vals: bfloat16 [384, 16, 128, 128], P(('col', 'layer'), 'row'), may hold values from -0.0546875 to 0.0546875
- b_cols: int32 [384, 16], P(('col', 'layer'), 'row'), may hold values from 0 to 31, as said below
- row_perm: int32 [64], replicated, may hold values from 0 to 63, as said below
Outputs:
- product: float32 [64, 32, 128, 128], P('row', ('col', 'layer'))
Inputs may be any that keep to these rules, and one draw needn't show every extreme that they name: `a_cols`: within each left tile row and inner range the 12 entries are distinct. `b_cols`: within each right tile row the 16 entries are distinct. `row_perm`: a permutation; the 8 product rows of each index of row take exactly 1 left rows from each aligned block of 8 left rows.
All inputs are finite; a program needn't handle non-finite values.
Results may differ from a plain program's by a relative error of at most 0.0003.
Values may be sent and summed in bfloat16 or wider, within the bound.
A program may use at most 192 MiB of HBM per device.

v0:
```python
import jax
import jax.numpy as jnp
from jax import lax
from jax.sharding import PartitionSpec as P

NC = 32


def sum_ranges(partial_value):
    return lax.psum_scatter(partial_value, ("col", "layer"), scatter_dimension=1, tiled=True)


def on_device(a_vals, a_cols, b_vals, b_cols, row_perm):
    count_rows = lax.axis_size("row")
    own_row = lax.axis_index("row")
    rows_here = a_vals.shape[0]
    tile = a_vals.shape[-1]
    group = rows_here // count_rows
    b_whole, bc_whole = (
        lax.all_gather(b_vals, "row", axis=1, tiled=True),
        lax.all_gather(b_cols, "row", axis=1, tiled=True),
    )
    slots_all = bc_whole.shape[1]
    taken = a_cols.shape[2]
    perm_table = row_perm.reshape(count_rows, rows_here)
    from_here = perm_table // rows_here == own_row
    send_order = jnp.argsort(jnp.where(from_here, 0, 1).astype(jnp.int32), axis=1, stable=True)[
        :, :group
    ]
    send_rows = (jnp.take_along_axis(perm_table, send_order, axis=1) % rows_here).reshape(rows_here)
    my_sources = lax.dynamic_slice_in_dim(row_perm, own_row * rows_here, rows_here) // rows_here
    source_hot = (my_sources[:, None] == jnp.arange(count_rows, dtype=jnp.int32)[None, :]).astype(
        jnp.int32
    )
    rank_within = jnp.sum((jnp.cumsum(source_hot, axis=0) - 1) * source_hot, axis=1)
    arrival = my_sources * group + rank_within
    send_vals = jnp.take(a_vals, send_rows, axis=0)
    send_cols = jnp.take(a_cols, send_rows, axis=0)
    recv_vals, recv_cols = (
        lax.all_to_all(send_vals, "row", split_axis=0, concat_axis=0, tiled=True),
        lax.all_to_all(send_cols, "row", split_axis=0, concat_axis=0, tiled=True),
    )
    left_vals = jnp.take(recv_vals, arrival, axis=0)[:, 0]
    left_cols = jnp.take(recv_cols, arrival, axis=0)[:, 0]

    def one_row(pair):
        vals, cols = pair
        picked = jnp.take(b_whole, cols, axis=0)
        targets = jnp.take(bc_whole, cols, axis=0).reshape(-1)
        prods = jnp.einsum("kab,kmbc->kmac", vals, picked, preferred_element_type=jnp.float32)
        prods = prods.reshape(taken * slots_all, tile, tile)
        return jnp.zeros((NC, tile, tile), jnp.float32).at[targets].add(prods)

    return sum_ranges(lax.map(one_row, (left_vals, left_cols)))


def solution(mesh):
    placed = (
        P("row", ("col", "layer"), None, None, None),
        P("row", ("col", "layer"), None),
        P(("col", "layer"), "row", None, None),
        P(("col", "layer"), "row"),
        P(),
    )
    return jax.shard_map(
        on_device,
        mesh=mesh,
        in_specs=placed,
        out_specs=P("row", ("col", "layer"), None, None),
        check_vma=False,
    )
```

profile of v0, /device:TPU:1, one launch (start us, length us, event | category | flops | bytes accessed | tf_op | source)
XLA Modules:
  0.0 813.0 jit_solution(11364405950228862627)
XLA Ops:
  29.6 75.0 %all-gather = s32[8,2,24]{2,1,0:T(2,128)S(1)} all-gather(s32[1,2,24]{2,1,0:T(2,128)S(1)} %bitcast.89), channel_id=1, replica_groups=mesh['row'=8,'col'=4,'layer'=4] {'row'}, dimensions={0}, use_global_device_ids=true | all-gather | bytes 1728 | tf_op jit(solution)/shard_map/all_gather | solution.py:21
  113.8 469.7 %while.10 = (s32[]{:T(128)}, f32[8,32,128,128]{3,2,1,0:T(8,128)}, s32[8,12]{1,0:T(8,128)S(1)}, s32[24,16]{1,0:T(8,128)S(1)}, bf16[24,16,128,128]{3,2,1,0:T(8,128...) while((s32[]{:T(128)}, f32[8,32,128,128]{3,2,1,0:T(8,128)}, s32[8,12]{1,0:T(8,128)S(1)}, ...), condition=%wide.region_5.8_spmd, body=%wide.region_3.7_spmd.sunk | while | flops 811599744 | bytes 101068968 | solution.py:54
  122.7 9.3 %fusion.26 = f32[12,16,128,128]{3,2,1,0:T(8,128)} fusion(bf16[12,16,128,128]{3,2,1,0:T(8,128)(2,1)} %gather_fusion.1, pred[12]{0:T(512)(128)(4,1)S(1)} %compare_and_fusion.4, bf16[8,12,128,128]{3,2,1,0:T(8,128)(2,1)} %get-tuple-element.116, s32[]{:T(128)} %get-tuple-element.103), kind=kOutput, calls=%fused_computation.8.clone.1 | convolution fusion | flops 808452096 | bytes 19268108 | tf_op jit(solution)/shard_map/while/body/eval_jaxpr/kab,kmbc->kmac/dot_general | solution.py:50
  132.0 12.7 %copy.29 = f32[192,128,128]{2,1,0:T(8,128)} copy(f32[192,128,128]{1,2,0:T(8,128)} %bitcast.82) | data formatting | bytes 25165824 | tf_op jit(solution)/shard_map/while/body/eval_jaxpr/reshape | solution.py:51
  145.6 25.4 %scatter_fusion = f32[32,128,128]{2,1,0:T(8,128)S(1)} fusion(f32[32,128,128]{2,1,0:T(8,128)S(1)} %broadcast.281, s32[192]{0:T(256)S(1)} %bitcast.87, f32[192,128,128]{2,1,0:T(8,128)} %copy.29), kind=kCustom, calls=%fused_computation.7.clone.1 | custom fusion | flops 3145728 | bytes 37749504 | tf_op jit(solution)/shard_map/while/body/eval_jaxpr/scatter-add | solution.py:52
  181.4 9.3 %fusion.26 = f32[12,16,128,128]{3,2,1,0:T(8,128)} fusion(bf16[12,16,128,128]{3,2,1,0:T(8,128)(2,1)} %gather_fusion.1, pred[12]{0:T(512)(128)(4,1)S(1)} %compare_and_fusion.4, bf16[8,12,128,128]{3,2,1,0:T(8,128)(2,1)} %get-tuple-element.116, s32[]{:T(128)} %get-tuple-element.103), kind=kOutput, calls=%fused_computation.8.clone.1 | convolution fusion | flops 808452096 | bytes 19268108 | tf_op jit(solution)/shard_map/while/body/eval_jaxpr/kab,kmbc->kmac/dot_general | solution.py:50
  190.7 12.7 %copy.29 = f32[192,128,128]{2,1,0:T(8,128)} copy(f32[192,128,128]{1,2,0:T(8,128)} %bitcast.82) | data formatting | bytes 25165824 | tf_op jit(solution)/shard_map/while/body/eval_jaxpr/reshape | solution.py:51
  204.3 25.4 %scatter_fusion = f32[32,128,128]{2,1,0:T(8,128)S(1)} fusion(f32[32,128,128]{2,1,0:T(8,128)S(1)} %broadcast.281, s32[192]{0:T(256)S(1)} %bitcast.87, f32[192,128,128]{2,1,0:T(8,128)} %copy.29), kind=kCustom, calls=%fused_computation.7.clone.1 | custom fusion | flops 3145728 | bytes 37749504 | tf_op jit(solution)/shard_map/while/body/eval_jaxpr/scatter-add | solution.py:52
  240.0 9.3 %fusion.26 = f32[12,16,128,128]{3,2,1,0:T(8,128)} fusion(bf16[12,16,128,128]{3,2,1,0:T(8,128)(2,1)} %gather_fusion.1, pred[12]{0:T(512)(128)(4,1)S(1)} %compare_and_fusion.4, bf16[8,12,128,128]{3,2,1,0:T(8,128)(2,1)} %get-tuple-element.116, s32[]{:T(128)} %get-tuple-element.103), kind=kOutput, calls=%fused_computation.8.clone.1 | convolution fusion | flops 808452096 | bytes 19268108 | tf_op jit(solution)/shard_map/while/body/eval_jaxpr/kab,kmbc->kmac/dot_general | solution.py:50
  249.3 12.7 %copy.29 = f32[192,128,128]{2,1,0:T(8,128)} copy(f32[192,128,128]{1,2,0:T(8,128)} %bitcast.82) | data formatting | bytes 25165824 | tf_op jit(solution)/shard_map/while/body/eval_jaxpr/reshape | solution.py:51
  263.0 25.4 %scatter_fusion = f32[32,128,128]{2,1,0:T(8,128)S(1)} fusion(f32[32,128,128]{2,1,0:T(8,128)S(1)} %broadcast.281, s32[192]{0:T(256)S(1)} %bitcast.87, f32[192,128,128]{2,1,0:T(8,128)} %copy.29), kind=kCustom, calls=%fused_computation.7.clone.1 | custom fusion | flops 3145728 | bytes 37749504 | tf_op jit(solution)/shard_map/while/body/eval_jaxpr/scatter-add | solution.py:52
  298.7 9.3 %fusion.26 = f32[12,16,128,128]{3,2,1,0:T(8,128)} fusion(bf16[12,16,128,128]{3,2,1,0:T(8,128)(2,1)} %gather_fusion.1, pred[12]{0:T(512)(128)(4,1)S(1)} %compare_and_fusion.4, bf16[8,12,128,128]{3,2,1,0:T(8,128)(2,1)} %get-tuple-element.116, s32[]{:T(128)} %get-tuple-element.103), kind=kOutput, calls=%fused_computation.8.clone.1 | convolution fusion | flops 808452096 | bytes 19268108 | tf_op jit(solution)/shard_map/while/body/eval_jaxpr/kab,kmbc->kmac/dot_general | solution.py:50
  308.0 12.7 %copy.29 = f32[192,128,128]{2,1,0:T(8,128)} copy(f32[192,128,128]{1,2,0:T(8,128)} %bitcast.82) | data formatting | bytes 25165824 | tf_op jit(solution)/shard_map/while/body/eval_jaxpr/reshape | solution.py:51
  321.7 25.4 %scatter_fusion = f32[32,128,128]{2,1,0:T(8,128)S(1)} fusion(f32[32,128,128]{2,1,0:T(8,128)S(1)} %broadcast.281, s32[192]{0:T(256)S(1)} %bitcast.87, f32[192,128,128]{2,1,0:T(8,128)} %copy.29), kind=kCustom, calls=%fused_computation.7.clone.1 | custom fusion | flops 3145728 | bytes 37749504 | tf_op jit(solution)/shard_map/while/body/eval_jaxpr/scatter-add | solution.py:52
  357.5 9.3 %fusion.26 = f32[12,16,128,128]{3,2,1,0:T(8,128)} fusion(bf16[12,16,128,128]{3,2,1,0:T(8,128)(2,1)} %gather_fusion.1, pred[12]{0:T(512)(128)(4,1)S(1)} %compare_and_fusion.4, bf16[8,12,128,128]{3,2,1,0:T(8,128)(2,1)} %get-tuple-element.116, s32[]{:T(128)} %get-tuple-element.103), kind=kOutput, calls=%fused_computation.8.clone.1 | convolution fusion | flops 808452096 | bytes 19268108 | tf_op jit(solution)/shard_map/while/body/eval_jaxpr/kab,kmbc->kmac/dot_general | solution.py:50
  366.8 12.7 %copy.29 = f32[192,128,128]{2,1,0:T(8,128)} copy(f32[192,128,128]{1,2,0:T(8,128)} %bitcast.82) | data formatting | bytes 25165824 | tf_op jit(solution)/shard_map/while/body/eval_jaxpr/reshape | solution.py:51
  380.4 25.4 %scatter_fusion = f32[32,128,128]{2,1,0:T(8,128)S(1)} fusion(f32[32,128,128]{2,1,0:T(8,128)S(1)} %broadcast.281, s32[192]{0:T(256)S(1)} %bitcast.87, f32[192,128,128]{2,1,0:T(8,128)} %copy.29), kind=kCustom, calls=%fused_computation.7.clone.1 | custom fusion | flops 3145728 | bytes 37749504 | tf_op jit(solution)/shard_map/while/body/eval_jaxpr/scatter-add | solution.py:52
  425.5 12.7 %copy.29 = f32[192,128,128]{2,1,0:T(8,128)} copy(f32[192,128,128]{1,2,0:T(8,128)} %bitcast.82) | data formatting | bytes 25165824 | tf_op jit(solution)/shard_map/while/body/eval_jaxpr/reshape | solution.py:51
  439.1 25.4 %scatter_fusion = f32[32,128,128]{2,1,0:T(8,128)S(1)} fusion(f32[32,128,128]{2,1,0:T(8,128)S(1)} %broadcast.281, s32[192]{0:T(256)S(1)} %bitcast.87, f32[192,128,128]{2,1,0:T(8,128)} %copy.29), kind=kCustom, calls=%fused_computation.7.clone.1 | custom fusion | flops 3145728 | bytes 37749504 | tf_op jit(solution)/shard_map/while/body/eval_jaxpr/scatter-add | solution.py:52
  484.2 12.7 %copy.29 = f32[192,128,128]{2,1,0:T(8,128)} copy(f32[192,128,128]{1,2,0:T(8,128)} %bitcast.82) | data formatting | bytes 25165824 | tf_op jit(solution)/shard_map/while/body/eval_jaxpr/reshape | solution.py:51
  497.8 25.4 %scatter_fusion = f32[32,128,128]{2,1,0:T(8,128)S(1)} fusion(f32[32,128,128]{2,1,0:T(8,128)S(1)} %broadcast.281, s32[192]{0:T(256)S(1)} %bitcast.87, f32[192,128,128]{2,1,0:T(8,128)} %copy.29), kind=kCustom, calls=%fused_computation.7.clone.1 | custom fusion | flops 3145728 | bytes 37749504 | tf_op jit(solution)/shard_map/while/body/eval_jaxpr/scatter-add | solution.py:52
  542.9 12.7 %copy.29 = f32[192,128,128]{2,1,0:T(8,128)} copy(f32[192,128,128]{1,2,0:T(8,128)} %bitcast.82) | data formatting | bytes 25165824 | tf_op jit(solution)/shard_map/while/body/eval_jaxpr/reshape | solution.py:51
  556.6 25.4 %scatter_fusion = f32[32,128,128]{2,1,0:T(8,128)S(1)} fusion(f32[32,128,128]{2,1,0:T(8,128)S(1)} %broadcast.281, s32[192]{0:T(256)S(1)} %bitcast.87, f32[192,128,128]{2,1,0:T(8,128)} %copy.29), kind=kCustom, calls=%fused_computation.7.clone.1 | custom fusion | flops 3145728 | bytes 37749504 | tf_op jit(solution)/shard_map/while/body/eval_jaxpr/scatter-add | solution.py:52
  585.4 218.5 %all-reduce.3.cloned.1.call-done = f32[8,32,128,128]{3,2,1,0:T(8,128)} async-done(((f32[8,32,128,128]{3,2,1,0:T(8,128)}), f32[8,32,128,128]{3,2,1,0:T(8,128)}) %all-reduce.3.cloned.1.call-update) | async-done | bytes 16777232
  (132 shorter events, 154.6 us)
Async XLA Ops:
  6.5 11.0 %copy-start = (bf16[8,1,12,128,128]{4,3,2,1,0:T(8,128)(2,1)S(1)}, bf16[8,1,12,128,128]{4,3,2,1,0:T(8,128)(2,1)}, u32[]{:S(2)}) copy-start(bf16[8,1,12,128,128]{4,3,2,1,0:T(8,128)(2,1)} %param.11) | copy-start | bytes 9437188
  6.5 107.2 %all-gather.3.cloned.1.call-start = ((), (), s32[]{:S(2)}) async-start(), calls=%async_computation.2 | async-start | bytes 14155776 | tf_op jit(solution)/shard_map/all_gather | solution.py:20
  11.6 12.9 %all-to-all-start = ((s32[8,1,12]{2,1,0:T(1,128)}), s32[8,1,12]{2,1,0:T(1,128)S(1)}, u32[]{:S(2)}, u32[]{:S(2)}) async-start(s32[8,1,12]{2,1,0:T(1,128)} %bitcast.17), calls=%async_computation | async-start | bytes 8192 | tf_op jit(solution)/shard_map/all_to_all | solution.py:41
  24.4 5.0 copy-start.2
  24.4 5.2 copy-start.3
  24.4 81.0 %all-to-all-start.1 = ((bf16[8,1,12,128,128]{4,3,2,1,0:T(8,128)(2,1)}), bf16[8,1,12,128,128]{4,3,2,1,0:T(8,128)(2,1)S(1)}, u32[]{:S(2)}, u32[]{:S(2)}) async-start(bf16[8,1,12,128,128]{4,3,2,1,0:T(8,128)(2,1)} %bitcast_select_fusion.1), calls=%async_computation.1 | async-start | bytes 6291456 | tf_op jit(solution)/shard_map/all_to_all | solution.py:40
  29.4 774.5 %all-reduce.3.cloned.1.call-start = ((), (), s32[]{:S(2)}) async-start(), calls=%async_computation.3 | async-start | bytes 33554432
  583.5 0.7 copy-start.4
  583.5 222.7 %copy-start.1 = (bf16[8,1,12,128,128]{4,3,2,1,0:T(8,128)(2,1)S(1)}, bf16[8,1,12,128,128]{4,3,2,1,0:T(8,128)(2,1)}, u32[]{:S(2)}) copy-start(bf16[8,1,12,128,128]{4,3,2,1,0:T(8,128)(2,1)} %param.11) | copy-start | bytes 9437188
Sparse Core Ops, SparseCore 0:
  9.1 104.6 all-gather.2
  583.6 220.2 all-reduce.2
where the time goes:
time: 818 us; the launch traced here: 813 us
  waiting for transfers between devices  221 us (27%)
  other arithmetic  214 us (26%)
  local copies, waits for them, and re-layouts  204 us (25%)
  blocking collectives  75 us (9%)
  matrix products  74.4 us (9%)
  between operations  14.1 us (2%)
  starting transfers between devices  10.9 us (1%)
    unnamed x3, waiting for transfers between devices  219 us
    scatter-add x8, other arithmetic, one_row(): return jnp.zeros((NC, tile, tile), jnp.float32).at[targets].add(prods)  203 us
    reshape x8, local copies, waits for them, and re-layouts, one_row(): prods = prods.reshape(taken * slots_all, tile, tile)  101 us
    all_gather x1, blocking collectives, on_device(): lax.all_gather(b_cols, 'row', axis=1, tiled=True)  75 us
    dot_general x8, matrix products, one_row(): jnp.einsum('kab,kmbc->kmac', vals, picked, preferred_element_type=jnp.flo...  74.4 us
    gather x8, local copies, waits for them, and re-layouts, one_row(): picked = jnp.take(b_whole, cols, axis=0)  70.7 us
  transfers between devices with their start and end apart: 4, of which 2 were waited for; matrix products, arithmetic and copies ran while one was open for 2% of the time, Pallas kernels for 0%

commit v1 on v0

v1 whole, which is shorter than its diff:
```python
import functools

import jax
import jax.numpy as jnp
from jax import lax
from jax.experimental import pallas as pl
from jax.experimental.pallas import tpu as pltpu
from jax.sharding import PartitionSpec as P

TILE = 128
NC = 32
KWR = 24
KA = 12
ROWS = 8
RING = 4
CHUNK = 4
NCH = KWR // CHUNK
PIECE = CHUNK * 2
HALF = PIECE // 2
NB = 256
TOP = 32767.0
PHASES = (2, 1, 3, 0)
MESH = pl.DeviceIdType.MESH


def encode(v):
    top = jnp.maximum(jnp.max(jnp.abs(v), axis=0, keepdims=True), 1e-30)
    coded = jnp.round(v * (TOP / top)).astype(jnp.int32).astype(jnp.int16)
    return coded, top * (1.0 / TOP)


def decode(coded, scale):
    return coded.astype(jnp.int32).astype(jnp.float32) * scale


def kernel(
    ia, ib, a_hbm, b_hbm, out,
    a_v, b_v0, b_v1, b_v2, b_v3, b_v4, b_v5, ad, bd, acc,
    s1, s1s, r1, r1s, s2, s2s, r2, r2s, s3, s3s, r3, r3s, fin,
    g_send, g_recv, loc_sem, m_send, m_recv, y_send, y_recv,
):
    b_v = (b_v0, b_v1, b_v2, b_v3, b_v4, b_v5)
    row = lax.axis_index("row")
    x = lax.axis_index("col")
    z = lax.axis_index("layer")
    y, c = row // 2, lax.rem(row, 2)

    def at_row(dy, dc):
        return lax.rem(y + dy, RING) * 2 + lax.rem(c + dc, 2)

    def dev_row(dy, dc):
        return (at_row(dy, dc), x, z)

    def dev_f(h, df):
        if h == 0:
            return (row, lax.rem(x + df, RING), z)
        return (row, x, lax.rem(z + df, RING))

    barrier = pltpu.get_barrier_semaphore()
    peers = [dev_row(dy, dc) for dy in range(RING) for dc in range(2) if dy or dc]
    peers += [dev_f(h, df) for h in range(2) for df in range(1, RING)]
    for peer in peers:
        pl.semaphore_signal(barrier, inc=1, device_id=peer, device_id_type=MESH)

    a_copy = pltpu.make_async_copy(a_hbm, a_v.at[pl.ds(0, ROWS * KA)], loc_sem.at[NCH])
    a_copy.start()
    own = [
        pltpu.make_async_copy(
            b_hbm.at[pl.ds(q * PIECE, PIECE)], b_v[q].at[pl.ds(row * PIECE, PIECE)], loc_sem.at[q]
        )
        for q in range(NCH)
    ]
    for q in range(NCH):
        own[q].start()
    zero = jnp.zeros((TILE, TILE), jnp.bfloat16)
    a_v[ROWS * KA] = zero
    for q in range(NCH):
        b_v[q][ROWS * PIECE] = zero
    pl.semaphore_wait(barrier, len(peers))

    def g_copy(q, kind, src, dst_at, n, target):
        return pltpu.make_async_remote_copy(
            src_ref=src,
            dst_ref=b_v[q].at[pl.ds(dst_at, n)],
            send_sem=g_send.at[q, kind],
            recv_sem=g_recv.at[q, kind],
            device_id=target,
            device_id_type=MESH,
        )

    up, down, sib = dev_row(1, 0), dev_row(3, 0), dev_row(0, 1)
    at_own, at_below, at_above, at_far = (at_row(d, 0) * PIECE for d in (0, 3, 1, 2))

    def g_all(q):
        mine = b_hbm.at[pl.ds(q * PIECE, PIECE)]
        held = lambda at, n: b_v[q].at[pl.ds(at, n)]
        return (
            g_copy(q, 0, mine, at_own, PIECE, up),
            g_copy(q, 1, mine, at_own, PIECE, down),
            g_copy(q, 2, mine, at_own, PIECE, sib),
            g_copy(q, 3, held(at_below, HALF), at_below, HALF, up),
            g_copy(q, 4, held(at_above + HALF, HALF), at_above + HALF, HALF, down),
            g_copy(q, 5, held(at_below, PIECE), at_below, PIECE, sib),
            g_copy(q, 6, held(at_above, PIECE), at_above, PIECE, sib),
            g_copy(q, 7, held(at_far, HALF), at_far, HALF, sib),
            g_copy(q, 8, held(at_far + HALF, HALF), at_far + HALF, HALF, sib),
        )

    copies = [g_all(q) for q in range(NCH)]

    def first(q):
        for kind in (0, 1, 2):
            copies[q][kind].start()

    def relay(q):
        copies[q][0].wait_recv()
        copies[q][3].start()
        copies[q][5].start()
        copies[q][1].wait_recv()
        copies[q][4].start()
        copies[q][6].start()

    def pass_on(q):
        copies[q][3].wait_recv()
        copies[q][7].start()
        copies[q][4].wait_recv()
        copies[q][8].start()

    def arrived(q):
        own[q].wait()
        for kind in (2, 5, 6, 7, 8):
            copies[q][kind].wait_recv()

    def dense_a(q):
        for t, dy in enumerate(PHASES):
            for h in range(2):
                d = 2 * t + h
                base = at_row(dy, h) * KWR + q * CHUNK
                for k in range(CHUNK):
                    ad[d * TILE : (d + 1) * TILE, k * TILE : (k + 1) * TILE] = a_v[ia[base + k]]

    def dense_b(q):
        for k in range(CHUNK):

            @pl.loop(0, NC, unroll=8)
            def _(col):
                at = pl.multiple_of(col * TILE, TILE)
                bd[k * TILE : (k + 1) * TILE, pl.ds(at, TILE)] = b_v[q][
                    ib[(q * CHUNK + k) * NC + col]
                ]

    def multiply(r0, r1_, n0, n1, begin):
        @pl.loop(n0, n1)
        def _(n):
            cols = pl.ds(pl.multiple_of(n * NB, NB), NB)
            part = jnp.dot(ad[r0:r1_, :], bd[:, cols], preferred_element_type=jnp.float32)
            if begin:
                acc[r0:r1_, cols] = part
            else:
                acc[r0:r1_, cols] = acc[r0:r1_, cols] + part

    def pos(h):
        return (x, z) if h == 0 else (z, x)

    def block(h, f_at, s_at):
        return f_at * RING + s_at if h == 0 else s_at * RING + f_at

    def held_tile(d, h, f_at, s_at, cc):
        lanes = pl.ds(pl.multiple_of(block(h, f_at, s_at) * 2 * TILE + cc * TILE, TILE), TILE)
        return (slice(d * TILE, (d + 1) * TILE), lanes)

    def m_copy(d, kind, src, dst, target):
        return pltpu.make_async_remote_copy(
            src_ref=src,
            dst_ref=dst,
            send_sem=m_send.at[d, kind],
            recv_sem=m_recv.at[d, kind],
            device_id=target,
            device_id_type=MESH,
        )

    def m_all(d, h):
        res = []
        for way in range(2):
            target = dev_f(h, 1 if way == 0 else 3)
            res.append(m_copy(d, 2 * way, s1.at[d, way], r1.at[d, way], target))
            res.append(m_copy(d, 2 * way + 1, s1s.at[d, way], r1s.at[d, way], target))
        for way in range(2):
            target = dev_f(h, 1 if way == 0 else 3)
            res.append(m_copy(d, 4 + 2 * way, s2.at[d, way], r2.at[d, way], target))
            res.append(m_copy(d, 5 + 2 * way, s2s.at[d, way], r2s.at[d, way], target))
        for ds in range(1, RING):
            target = dev_f(1 - h, ds)
            res.append(m_copy(d, 6 + 2 * ds, s3.at[d, ds - 1], r3.at[d, ds - 1], target))
            res.append(m_copy(d, 7 + 2 * ds, s3s.at[d, ds - 1], r3s.at[d, ds - 1], target))
        return res

    m = [m_all(d, d % 2) for d in range(ROWS)]

    def far_part(d):
        h = d % 2
        f, _ = pos(h)
        f2 = lax.rem(f + 2, RING)
        for way in range(2):

            @pl.loop(0, 4)
            def _(i):
                v = acc[held_tile(d, h, f2, way * 2 + i // 2, lax.rem(i, 2))]
                coded, scale = encode(v)
                s1[d, way, i] = coded
                s1s[d, way, pl.ds(i, 1), :] = scale

            m[d][2 * way].start()
            m[d][2 * way + 1].start()

    def near_part(d):
        h = d % 2
        f, _ = pos(h)
        for way in range(2):
            fd = lax.rem(f + (1 if way == 0 else 3), RING)
            m[d][2 * way].wait_recv()
            m[d][2 * way + 1].wait_recv()

            @pl.loop(0, 4)
            def _(i):
                v = acc[held_tile(d, h, fd, (1 - way) * 2 + i // 2, lax.rem(i, 2))]
                coded, scale = encode(v)
                s2[d, way, (1 - way) * 4 + i] = coded
                s2s[d, way, pl.ds((1 - way) * 4 + i, 1), :] = scale

            @pl.loop(0, 4)
            def _(i):
                v = acc[held_tile(d, h, fd, way * 2 + i // 2, lax.rem(i, 2))]
                v = v + decode(r1[d, way, i], r1s[d, way, pl.ds(i, 1), :])
                coded, scale = encode(v)
                s2[d, way, way * 4 + i] = coded
                s2s[d, way, pl.ds(way * 4 + i, 1), :] = scale

            m[d][4 + 2 * way].start()
            m[d][5 + 2 * way].start()

    def second(d):
        h = d % 2
        f, s = pos(h)
        for kind in range(4, 8):
            m[d][kind].wait_recv()
        for ds in (1, 2, 3, 0):
            s_at = lax.rem(s + ds, RING)

            @pl.loop(0, 2)
            def _(cc):
                where = held_tile(d, h, f, s_at, cc)
                i = s_at * 2 + cc
                v = (
                    acc[where]
                    + decode(r2[d, 0, i], r2s[d, 0, pl.ds(i, 1), :])
                    + decode(r2[d, 1, i], r2s[d, 1, pl.ds(i, 1), :])
                )
                if ds == 0:
                    fin[d, cc] = v
                else:
                    coded, scale = encode(v)
                    s3[d, ds - 1, cc] = coded
                    s3s[d, ds - 1, pl.ds(cc, 1), :] = scale

            if ds:
                m[d][6 + 2 * ds].start()
                m[d][7 + 2 * ds].start()

    y_copies = []
    for t, dy in enumerate(PHASES):
        for h in range(2):
            d = 2 * t + h
            if dy or h:
                y_copies.append(
                    pltpu.make_async_remote_copy(
                        src_ref=fin.at[d],
                        dst_ref=out.at[row],
                        send_sem=y_send.at[d],
                        recv_sem=y_recv.at[d],
                        device_id=dev_row(dy, h),
                        device_id_type=MESH,
                    )
                )
            else:
                y_copies.append(pltpu.make_async_copy(fin.at[d], out.at[row], y_send.at[d]))

    def last(d):
        for kind in range(8, 14):
            m[d][kind].wait_recv()

        @pl.loop(0, 2)
        def _(cc):
            v = fin[d, cc]
            for k in range(3):
                v = v + decode(r3[d, k, cc], r3s[d, k, pl.ds(cc, 1), :])
            fin[d, cc] = v

        y_copies[d].start()

    def both(step, t):
        step(2 * t)
        step(2 * t + 1)

    first(0)
    first(1)
    first(2)
    relay(0)
    pass_on(0)
    a_copy.wait()
    arrived(0)
    nsteps = NC * TILE // NB
    for q in range(NCH - 1):
        relay(q + 1)
        if q + 3 < NCH:
            first(q + 3)
        dense_a(q)
        dense_b(q)
        multiply(0, ROWS * TILE, 0, nsteps // 2, q == 0)
        pass_on(q + 1)
        multiply(0, ROWS * TILE, nsteps // 2, nsteps, q == 0)
        arrived(q + 1)
    dense_a(NCH - 1)
    dense_b(NCH - 1)

    def ready(t):
        multiply(2 * t * TILE, 2 * (t + 1) * TILE, 0, nsteps, False)
        both(far_part, t)

    ready(0)
    ready(1)
    both(near_part, 0)
    ready(2)
    both(near_part, 1)
    both(second, 0)
    ready(3)
    both(near_part, 2)
    both(second, 1)
    both(last, 0)
    both(near_part, 3)
    both(second, 2)
    both(last, 1)
    both(second, 3)
    both(last, 2)
    both(last, 3)

    for q in range(NCH):
        for copy in copies[q]:
            copy.wait_send()
    for d in range(ROWS):
        for copy in m[d]:
            copy.wait_send()
        t, h = d // 2, d % 2
        if PHASES[t] or h:
            y_copies[d].wait()
        else:
            y_copies[d].wait()


def exchange(ia, ib, a_vals, b_vals):
    bf16, f32, i16 = jnp.bfloat16, jnp.float32, jnp.int16
    t2 = (TILE, TILE)
    b_chunk = pltpu.VMEM((ROWS * PIECE + 1, *t2), bf16)
    dma = pltpu.SemaphoreType.DMA
    return pl.pallas_call(
        kernel,
        out_shape=jax.ShapeDtypeStruct((ROWS, 2, *t2), f32),
        in_specs=[
            pl.BlockSpec(memory_space=pltpu.SMEM),
            pl.BlockSpec(memory_space=pltpu.SMEM),
            pl.BlockSpec(memory_space=pl.ANY),
            pl.BlockSpec(memory_space=pl.ANY),
        ],
        out_specs=pl.BlockSpec(memory_space=pl.ANY),
        scratch_shapes=[
            pltpu.VMEM((ROWS * KA + 1, *t2), bf16),
            b_chunk, b_chunk, b_chunk, b_chunk, b_chunk, b_chunk,
            pltpu.VMEM((ROWS * TILE, CHUNK * TILE), bf16),
            pltpu.VMEM((CHUNK * TILE, NC * TILE), bf16),
            pltpu.VMEM((ROWS * TILE, NC * TILE), f32),
            pltpu.VMEM((ROWS, 2, 4, *t2), i16),
            pltpu.VMEM((ROWS, 2, 8, TILE), f32),
            pltpu.VMEM((ROWS, 2, 4, *t2), i16),
            pltpu.VMEM((ROWS, 2, 8, TILE), f32),
            pltpu.VMEM((ROWS, 2, 8, *t2), i16),
            pltpu.VMEM((ROWS, 2, 8, TILE), f32),
            pltpu.VMEM((ROWS, 2, 8, *t2), i16),
            pltpu.VMEM((ROWS, 2, 8, TILE), f32),
            pltpu.VMEM((ROWS, 3, 2, *t2), i16),
            pltpu.VMEM((ROWS, 3, 8, TILE), f32),
            pltpu.VMEM((ROWS, 3, 2, *t2), i16),
            pltpu.VMEM((ROWS, 3, 8, TILE), f32),
            pltpu.VMEM((ROWS, 2, *t2), f32),
            dma((NCH, 9)), dma((NCH, 9)), dma((NCH + 1,)),
            dma((ROWS, 14)), dma((ROWS, 14)), dma((ROWS,)), dma((ROWS,)),
        ],
        compiler_params=pltpu.CompilerParams(
            collective_id=0, has_side_effects=True, vmem_limit_bytes=60 * 1024 * 1024
        ),
        name="exchange",
    )(ia, ib, a_vals, b_vals)


def on_device(a_vals, a_cols, b_vals, b_cols, row_perm):
    own_row = lax.axis_index("row")
    i32 = jnp.int32
    perm = row_perm.reshape(ROWS, ROWS)
    taken = jnp.sum(jnp.where(perm // ROWS == own_row, perm % ROWS, 0), axis=1)
    hot_row = taken[:, None] == jnp.arange(ROWS, dtype=i32)[None, :]
    cols = jnp.sum(jnp.where(hot_row[:, :, None], a_cols[:, 0][None], 0), axis=1)
    hot = cols[:, :, None] == jnp.arange(KWR, dtype=i32)
    at = taken[:, None] * KA + jnp.arange(KA, dtype=i32)[None, :]
    none = ROWS * KA
    ia = none + jnp.sum(jnp.where(hot, at[:, :, None] - none, 0), axis=1)
    bc = lax.all_gather(b_cols, "row", axis=1, tiled=True)
    slot = jnp.arange(2 * ROWS, dtype=i32)[None, :]
    r = jnp.arange(KWR, dtype=i32)[:, None]
    at = slot // 2 * PIECE + r % CHUNK * 2 + slot % 2
    none = ROWS * PIECE
    hot = bc[:, :, None] == jnp.arange(NC, dtype=i32)
    ib = none + jnp.sum(jnp.where(hot, at[:, :, None] - none, 0), axis=1)
    got = exchange(
        ia.reshape(-1),
        ib.reshape(-1),
        a_vals.reshape(ROWS * KA, TILE, TILE),
        b_vals.reshape(KWR * 2, TILE, TILE),
    )
    source = lax.dynamic_slice_in_dim(row_perm, own_row * ROWS, ROWS) // ROWS
    return jnp.take(got, source, axis=0)


def solution(mesh):
    placed = (
        P("row", ("col", "layer"), None, None, None),
        P("row", ("col", "layer"), None),
        P(("col", "layer"), "row", None, None),
        P(("col", "layer"), "row"),
        P(),
    )
    return jax.shard_map(
        on_device,
        mesh=mesh,
        in_specs=placed,
        out_specs=P("row", ("col", "layer"), None, None),
        check_vma=False,
    )
```

time: 818 us -> 156 us (0.19)
  waiting for transfers between devices: 221 us -> 0 us
  other arithmetic: 214 us -> 3.23 us
  local copies, waits for them, and re-layouts: 204 us -> 4.06 us
  Pallas kernels: 0 us -> 136 us
  matrix products: 74.4 us -> 0 us
  blocking collectives: 75 us -> 12.4 us
  between operations: 14.1 us -> 0.07 us
  starting transfers between devices: 10.9 us -> 0 us
    unnamed x3 -> x0, waiting for transfers between devices: 219 us -> none
    scatter-add x8 -> x0, other arithmetic: 203 us -> none  [one_row(): return jnp.zeros((NC, tile, tile), jnp.float32).at[targets].add(prods)]
    pallas_call x0 -> x1, Pallas kernels: none -> 136 us  [exchange(): pl.pallas_call(kernel, out_shape=jax.ShapeDtypeStruct((ROWS, 2, *t2), f32...]
    reshape x10 -> x1, local copies, waits for them, and re-layouts: 102 us -> 0.73 us  [on_device(): perm = row_perm.reshape(ROWS, ROWS)]
    gather x21 -> x1, local copies, waits for them, and re-layouts: 82.8 us -> 1.84 us  [on_device(): return jnp.take(got, source, axis=0)]
    dot_general x8 -> x0, matrix products: 74.4 us -> none  [one_row(): jnp.einsum('kab,kmbc->kmac', vals, picked, preferred_element_type=jnp.flo...]
    all_gather x1, blocking collectives: 75 us -> 12.4 us  [on_device(): bc = lax.all_gather(b_cols, 'row', axis=1, tiled=True)]
    dynamic_update_slice x8 -> x0, local copies, waits for them, and re-layouts: 12.6 us -> none  [on_device(): return sum_ranges(lax.map(one_row, (left_vals, left_cols)))]
  transfers between devices with their start and end apart: 4 -> 0, of which waited for: 2 -> 0; matrix products, arithmetic and copies ran while one was open for 2% -> 0% of each run, Pallas kernels for 0% -> 0%
where the time goes in v1:
time: 156 us; the launch traced here: 155 us
  Pallas kernels  136 us (87%)
  blocking collectives  12.4 us (8%)
  local copies, waits for them, and re-layouts  4.06 us (3%)
  other arithmetic  3.23 us (2%)
    pallas_call x1, Pallas kernels, exchange(): pl.pallas_call(kernel, out_shape=jax.ShapeDtypeStruct((ROWS, 2, *t2), f32...  136 us
    all_gather x1, blocking collectives, on_device(): bc = lax.all_gather(b_cols, 'row', axis=1, tiled=True)  12.4 us

profile of v1, /device:TPU:1, one launch (start us, length us, event | category | flops | bytes accessed | tf_op | source)
XLA Modules:
  0.0 155.4 jit_solution(12266277534963256438)
XLA Ops:
  0.0 0.7 compare_and_fusion
  0.8 0.7 reshape.185
  1.5 0.1 fusion.2
  1.6 0.1 iota_compare_fusion.2
  1.7 0.8 select_reduce_fusion.2
  2.5 0.1 copy.8
  2.6 0.1 select_reduce_fusion.1
  2.7 0.7 add.129.ia
  3.4 12.4 %all-gather = s32[8,2,24]{2,1,0:T(2,128)S(1)} all-gather(s32[1,2,24]{2,1,0:T(2,128)} %bitcast.13), channel_id=1, replica_groups=mesh['row'=8,'col'=4,'layer'=4] {'row'}, dimensions={0}, use_global_device_ids=true | all-gather | bytes 1728 | tf_op jit(solution)/shard_map/all_gather | solution.py:415
  15.7 0.1 copy.9
  15.8 0.1 add_add_fusion
  15.9 0.2 select_reduce_fusion
  16.1 0.7 add.139.ib
  16.7 135.6 %exchange.1 = f32[8,2,128,128]{3,2,1,0:T(8,128)} custom-call(s32[192]{0:T(256)} %add.129.ia, s32[768]{0:T(1024)} %add.139.ib, bf16[96,128,128]{2,1,0:T(8,128)(2,1)} %bitcast.9, bf16[48,128,128]{2,1,0:T(8,128)(2,1)} %bitcast.10), custom_call_target="tpu_custom_call" | custom-call | tf_op jit(solution)/shard_map/exchange/pallas_call | solution.py:365
  152.4 1.8 %gather_fusion = f32[8,2,128,128]{3,2,1,0:T(8,128)S(1)} fusion(f32[8,2,128,128]{3,2,1,0:T(8,128)} %exchange.1, s32[1024]{0:T(1024)S(1)} %pad_clamp_fusion), kind=kCustom, calls=%fused_computation | custom fusion | bytes 2097184 | tf_op jit(solution)/shard_map/jit(_take)/gather | solution.py:429
  154.2 1.1 broadcast_select_fusion
  (7 shorter events, 0.0 us)

commit v2 on v1

--- a/solution.py
+++ b/solution.py
@@ -17,8 +17,10 @@
 NCH = KWR // CHUNK
 PIECE = CHUNK * 2
 HALF = PIECE // 2
-NB = 256
+NB = 1024
+NSTEP = NC * TILE // NB
 TOP = 32767.0
+UNROLL = 4
 PHASES = (2, 1, 3, 0)
 MESH = pl.DeviceIdType.MESH
 
@@ -34,10 +36,10 @@
 
 
 def kernel(
-    ia, ib, a_hbm, b_hbm, out,
-    a_v, b_v0, b_v1, b_v2, b_v3, b_v4, b_v5, ad, bd, acc,
+    perm, ac_ref, bc_ref, a_hbm, b_hbm, out,
+    a_v, b_v0, b_v1, b_v2, b_v3, b_v4, b_v5, ad, acc, ia_v, bc_v, ib_v, w_own, w_all, ia, ib,
     s1, s1s, r1, r1s, s2, s2s, r2, r2s, s3, s3s, r3, r3s, fin,
-    g_send, g_recv, loc_sem, m_send, m_recv, y_send, y_recv,
+    g_send, g_recv, loc_sem, w_send, w_recv, m_send, m_recv, y_send, y_recv,
 ):
     b_v = (b_v0, b_v1, b_v2, b_v3, b_v4, b_v5)
     row = lax.axis_index("row")
@@ -61,6 +63,23 @@
     peers += [dev_f(h, df) for h in range(2) for df in range(1, RING)]
     for peer in peers:
         pl.semaphore_signal(barrier, inc=1, device_id=peer, device_id_type=MESH)
+
+    lane = lax.broadcasted_iota(jnp.int32, (ROWS, TILE), 1)
+    left = lax.broadcasted_iota(jnp.int32, (ROWS, TILE), 0)
+    table = jnp.full((ROWS, TILE), ROWS * KA, jnp.int32)
+    for k in range(KA):
+        table = jnp.where(ac_ref[:, k : k + 1] == lane, left * KA + k, table)
+    ia_v[...] = table
+    ia_copy = pltpu.make_async_copy(ia_v, ia, loc_sem.at[NCH + 1])
+    ia_copy.start()
+    bc_v[...] = jnp.full((ROWS, TILE), -1, jnp.int32)
+    bc_v[0:2, 0:KWR] = bc_ref[...]
+    col = lax.broadcasted_iota(jnp.int32, (NC, TILE), 0)
+    inner = lax.rem(lax.broadcasted_iota(jnp.int32, (NC, TILE), 1), CHUNK)
+    table = jnp.zeros((NC, TILE), jnp.int32)
+    for k in range(2):
+        table = jnp.where(bc_v[k : k + 1, :] == col, row * PIECE + inner * 2 + k + 1, table)
+    w_own[...] = table
 
     a_copy = pltpu.make_async_copy(a_hbm, a_v.at[pl.ds(0, ROWS * KA)], loc_sem.at[NCH])
     a_copy.start()
@@ -78,6 +97,35 @@
         b_v[q][ROWS * PIECE] = zero
     pl.semaphore_wait(barrier, len(peers))
 
+    w_copies = [
+        pltpu.make_async_remote_copy(
+            src_ref=w_own,
+            dst_ref=w_all.at[row],
+            send_sem=w_send.at[2 * dy + dc],
+            recv_sem=w_recv.at[2 * dy + dc],
+            device_id=dev_row(dy, dc),
+            device_id_type=MESH,
+        )
+        for dy in range(RING)
+        for dc in range(2)
+        if dy or dc
+    ]
+    for copy in w_copies:
+        copy.start()
+
+    def tables():
+        w_all[row] = w_own[...]
+        for copy in w_copies:
+            copy.wait_recv()
+        top = w_all[0]
+        for source in range(1, ROWS):
+            top = jnp.maximum(top, w_all[source])
+        ib_v[...] = jnp.where(top > 0, top - 1, ROWS * PIECE)
+        ib_copy = pltpu.make_async_copy(ib_v, ib, loc_sem.at[NCH + 2])
+        ib_copy.start()
+        ib_copy.wait()
+        ia_copy.wait()
+
     def g_copy(q, kind, src, dst_at, n, target):
         return pltpu.make_async_remote_copy(
             src_ref=src,
@@ -131,30 +179,38 @@
         for kind in (2, 5, 6, 7, 8):
             copies[q][kind].wait_recv()
 
-    def dense_a(q):
-        for t, dy in enumerate(PHASES):
-            for h in range(2):
-                d = 2 * t + h
-                base = at_row(dy, h) * KWR + q * CHUNK
-                for k in range(CHUNK):
-                    ad[d * TILE : (d + 1) * TILE, k * TILE : (k + 1) * TILE] = a_v[ia[base + k]]
-
-    def dense_b(q):
-        for k in range(CHUNK):
-
-            @pl.loop(0, NC, unroll=8)
-            def _(col):
-                at = pl.multiple_of(col * TILE, TILE)
-                bd[k * TILE : (k + 1) * TILE, pl.ds(at, TILE)] = b_v[q][
-                    ib[(q * CHUNK + k) * NC + col]
+    def taken(j):
+        total = jnp.int32(0)
+        for i in range(ROWS):
+            p = perm[j * ROWS + i]
+            total = jnp.maximum(total, jnp.where(lax.div(p, ROWS) == row, lax.rem(p, ROWS), 0))
+        return total
+
+    def dense_a(q, rows):
+        for d in range(ROWS):
+            for k in range(CHUNK):
+                ad[d * TILE : (d + 1) * TILE, k * TILE : (k + 1) * TILE] = a_v[
+                    ia[rows[d], q * CHUNK + k]
                 ]
 
-    def multiply(r0, r1_, n0, n1, begin):
-        @pl.loop(n0, n1)
+    def multiply(q, r0, r1_, hooks=()):
+        @pl.loop(0, NSTEP)
         def _(n):
+            for step, act in hooks:
+                pl.when(n == step)(act)
+            wide = NB // TILE
+            right = jnp.concatenate(
+                [
+                    jnp.concatenate(
+                        [b_v[q][ib[n * wide + i, q * CHUNK + k]] for i in range(wide)], axis=1
+                    )
+                    for k in range(CHUNK)
+                ],
+                axis=0,
+            )
             cols = pl.ds(pl.multiple_of(n * NB, NB), NB)
-            part = jnp.dot(ad[r0:r1_, :], bd[:, cols], preferred_element_type=jnp.float32)
-            if begin:
+            part = jnp.dot(ad[r0:r1_, :], right, preferred_element_type=jnp.float32)
+            if q == 0:
                 acc[r0:r1_, cols] = part
             else:
                 acc[r0:r1_, cols] = acc[r0:r1_, cols] + part
@@ -203,7 +259,7 @@
         f2 = lax.rem(f + 2, RING)
         for way in range(2):
 
-            @pl.loop(0, 4)
+            @pl.loop(0, 4, unroll=UNROLL)
             def _(i):
                 v = acc[held_tile(d, h, f2, way * 2 + i // 2, lax.rem(i, 2))]
                 coded, scale = encode(v)
@@ -221,14 +277,14 @@
             m[d][2 * way].wait_recv()
             m[d][2 * way + 1].wait_recv()
 
-            @pl.loop(0, 4)
+            @pl.loop(0, 4, unroll=UNROLL)
             def _(i):
                 v = acc[held_tile(d, h, fd, (1 - way) * 2 + i // 2, lax.rem(i, 2))]
                 coded, scale = encode(v)
                 s2[d, way, (1 - way) * 4 + i] = coded
                 s2s[d, way, pl.ds((1 - way) * 4 + i, 1), :] = scale
 
-            @pl.loop(0, 4)
+            @pl.loop(0, 4, unroll=UNROLL)
             def _(i):
                 v = acc[held_tile(d, h, fd, way * 2 + i // 2, lax.rem(i, 2))]
                 v = v + decode(r1[d, way, i], r1s[d, way, pl.ds(i, 1), :])
@@ -247,7 +303,7 @@
         for ds in (1, 2, 3, 0):
             s_at = lax.rem(s + ds, RING)
 
-            @pl.loop(0, 2)
+            @pl.loop(0, 2, unroll=2)
             def _(cc):
                 where = held_tile(d, h, f, s_at, cc)
                 i = s_at * 2 + cc
@@ -289,7 +345,7 @@
         for kind in range(8, 14):
             m[d][kind].wait_recv()
 
-        @pl.loop(0, 2)
+        @pl.loop(0, 2, unroll=2)
         def _(cc):
             v = fin[d, cc]
             for k in range(3):
@@ -304,27 +360,36 @@
 
     first(0)
     first(1)
+    tables()
+    rows = [taken(at_row(dy, h)) for dy in PHASES for h in range(2)]
+    relay(0)
     first(2)
-    relay(0)
+    relay(1)
+    first(3)
     pass_on(0)
     a_copy.wait()
     arrived(0)
-    nsteps = NC * TILE // NB
     for q in range(NCH - 1):
-        relay(q + 1)
-        if q + 3 < NCH:
-            first(q + 3)
-        dense_a(q)
-        dense_b(q)
-        multiply(0, ROWS * TILE, 0, nsteps // 2, q == 0)
-        pass_on(q + 1)
-        multiply(0, ROWS * TILE, nsteps // 2, nsteps, q == 0)
+        dense_a(q, rows)
+        hooks = []
+        if q + 2 < NCH:
+
+            def onward(q=q):
+                relay(q + 2)
+                if q + 4 < NCH:
+                    first(q + 4)
+
+            hooks.append((NSTEP - 1, onward))
+        else:
+            hooks.append((NSTEP - 2, functools.partial(pass_on, q + 1)))
+        multiply(q, 0, ROWS * TILE, hooks)
+        if q + 2 < NCH:
+            pass_on(q + 1)
         arrived(q + 1)
-    dense_a(NCH - 1)
-    dense_b(NCH - 1)
+    dense_a(NCH - 1, rows)
 
     def ready(t):
-        multiply(2 * t * TILE, 2 * (t + 1) * TILE, 0, nsteps, False)
+        multiply(NCH - 1, 2 * t * TILE, 2 * (t + 1) * TILE)
         both(far_part, t)
 
     ready(0)
@@ -332,33 +397,31 @@
     both(near_part, 0)
     ready(2)
     both(near_part, 1)
-    both(second, 0)
     ready(3)
     both(near_part, 2)
+    both(second, 0)
+    both(near_part, 3)
     both(second, 1)
     both(last, 0)
-    both(near_part, 3)
     both(second, 2)
     both(last, 1)
     both(second, 3)
     both(last, 2)
     both(last, 3)
 
+    for copy in w_copies:
+        copy.wait_send()
     for q in range(NCH):
         for copy in copies[q]:
             copy.wait_send()
     for d in range(ROWS):
         for copy in m[d]:
             copy.wait_send()
-        t, h = d // 2, d % 2
-        if PHASES[t] or h:
-            y_copies[d].wait()
-        else:
-            y_copies[d].wait()
-
-
-def exchange(ia, ib, a_vals, b_vals):
-    bf16, f32, i16 = jnp.bfloat16, jnp.float32, jnp.int16
+        y_copies[d].wait()
+
+
+def exchange(row_perm, a_cols, b_cols, a_vals, b_vals):
+    bf16, f32, i16, i32 = jnp.bfloat16, jnp.float32, jnp.int16, jnp.int32
     t2 = (TILE, TILE)
     b_chunk = pltpu.VMEM((ROWS * PIECE + 1, *t2), bf16)
     dma = pltpu.SemaphoreType.DMA
@@ -367,7 +430,8 @@
         out_shape=jax.ShapeDtypeStruct((ROWS, 2, *t2), f32),
         in_specs=[
             pl.BlockSpec(memory_space=pltpu.SMEM),
-            pl.BlockSpec(memory_space=pltpu.SMEM),
+            pl.BlockSpec(memory_space=pltpu.VMEM),
+            pl.BlockSpec(memory_space=pltpu.VMEM),
             pl.BlockSpec(memory_space=pl.ANY),
             pl.BlockSpec(memory_space=pl.ANY),
         ],
@@ -376,8 +440,14 @@
             pltpu.VMEM((ROWS * KA + 1, *t2), bf16),
             b_chunk, b_chunk, b_chunk, b_chunk, b_chunk, b_chunk,
             pltpu.VMEM((ROWS * TILE, CHUNK * TILE), bf16),
-            pltpu.VMEM((CHUNK * TILE, NC * TILE), bf16),
             pltpu.VMEM((ROWS * TILE, NC * TILE), f32),
+            pltpu.VMEM((ROWS, TILE), i32),
+            pltpu.VMEM((ROWS, TILE), i32),
+            pltpu.VMEM((NC, TILE), i32),
+            pltpu.VMEM((NC, TILE), i32),
+            pltpu.VMEM((ROWS, NC, TILE), i32),
+            pltpu.SMEM((ROWS, TILE), i32),
+            pltpu.SMEM((NC, TILE), i32),
             pltpu.VMEM((ROWS, 2, 4, *t2), i16),
             pltpu.VMEM((ROWS, 2, 8, TILE), f32),
             pltpu.VMEM((ROWS, 2, 4, *t2), i16),
@@ -391,42 +461,27 @@
             pltpu.VMEM((ROWS, 3, 2, *t2), i16),
             pltpu.VMEM((ROWS, 3, 8, TILE), f32),
             pltpu.VMEM((ROWS, 2, *t2), f32),
-            dma((NCH, 9)), dma((NCH, 9)), dma((NCH + 1,)),
+            dma((NCH, 9)), dma((NCH, 9)), dma((NCH + 3,)), dma((ROWS,)), dma((ROWS,)),
             dma((ROWS, 14)), dma((ROWS, 14)), dma((ROWS,)), dma((ROWS,)),
         ],
         compiler_params=pltpu.CompilerParams(
             collective_id=0, has_side_effects=True, vmem_limit_bytes=60 * 1024 * 1024
         ),
         name="exchange",
-    )(ia, ib, a_vals, b_vals)
+    )(row_perm, a_cols, b_cols, a_vals, b_vals)
 
 
 def on_device(a_vals, a_cols, b_vals, b_cols, row_perm):
-    own_row = lax.axis_index("row")
-    i32 = jnp.int32
-    perm = row_perm.reshape(ROWS, ROWS)
-    taken = jnp.sum(jnp.where(perm // ROWS == own_row, perm % ROWS, 0), axis=1)
-    hot_row = taken[:, None] == jnp.arange(ROWS, dtype=i32)[None, :]
-    cols = jnp.sum(jnp.where(hot_row[:, :, None], a_cols[:, 0][None], 0), axis=1)
-    hot = cols[:, :, None] == jnp.arange(KWR, dtype=i32)
-    at = taken[:, None] * KA + jnp.arange(KA, dtype=i32)[None, :]
-    none = ROWS * KA
-    ia = none + jnp.sum(jnp.where(hot, at[:, :, None] - none, 0), axis=1)
-    bc = lax.all_gather(b_cols, "row", axis=1, tiled=True)
-    slot = jnp.arange(2 * ROWS, dtype=i32)[None, :]
-    r = jnp.arange(KWR, dtype=i32)[:, None]
-    at = slot // 2 * PIECE + r % CHUNK * 2 + slot % 2
-    none = ROWS * PIECE
-    hot = bc[:, :, None] == jnp.arange(NC, dtype=i32)
-    ib = none + jnp.sum(jnp.where(hot, at[:, :, None] - none, 0), axis=1)
     got = exchange(
-        ia.reshape(-1),
-        ib.reshape(-1),
+        row_perm,
+        a_cols.reshape(ROWS, KA),
+        b_cols.T,
         a_vals.reshape(ROWS * KA, TILE, TILE),
         b_vals.reshape(KWR * 2, TILE, TILE),
     )
+    own_row = lax.axis_index("row")
     source = lax.dynamic_slice_in_dim(row_perm, own_row * ROWS, ROWS) // ROWS
-    return jnp.take(got, source, axis=0)
+    return got.at[source].get(mode="promise_in_bounds")
 
 
 def solution(mesh):

time: 156 us -> 129 us (0.83)
  blocking collectives: 12.4 us -> 0 us
  Pallas kernels: 136 us -> 126 us
  other arithmetic: 3.23 us -> 0.74 us
    all_gather x1 -> x0, blocking collectives: 12.4 us -> none  [on_device(): bc = lax.all_gather(b_cols, 'row', axis=1, tiled=True)]
    pallas_call x1, Pallas kernels: 136 us -> 126 us  [exchange(): pl.pallas_call(kernel, out_shape=jax.ShapeDtypeStruct((ROWS, 2, *t2), f32...]
where the time goes in v2:
time: 129 us
  Pallas kernels  126 us (98%)
  local copies, waits for them, and re-layouts  2.81 us (2%)
    pallas_call x1, Pallas kernels, exchange(): pl.pallas_call(kernel, out_shape=jax.ShapeDtypeStruct((ROWS, 2, *t2), f32...  126 us
    gather x1, local copies, waits for them, and re-layouts, on_device(): return got.at[source].get(mode='promise_in_bounds')  2.81 us

profile of v2, /device:TPU:1, one launch (start us, length us, event | category | flops | bytes accessed | tf_op | source)
XLA Modules:
  0.0 129.3 jit_solution(16183593350611688896)
XLA Ops:
  0.0 0.7 compare_select_fusion
  0.7 125.7 %exchange.1 = f32[8,2,128,128]{3,2,1,0:T(8,128)} custom-call(s32[64]{0:T(128)} %perm.1, s32[8,12]{1,0:T(8,128)} %bitcast.6, s32[2,24]{1,0:T(2,128)} %bitcast.7, bf16[96,128,128]{2,1,0:T(8,128)(2,1)} %bitcast.4, bf16[48,128,128]{2,1,0:T(8,128)(2,1)} %bitcast.5), custom_call_target="tpu_custom_call" | custom-call | tf_op jit(solution)/shard_map/exchange/pallas_call | solution.py:428
  126.5 2.8 %gather_fusion = f32[8,2,128,128]{3,2,1,0:T(8,128)} fusion(f32[8,2,128,128]{3,2,1,0:T(8,128)} %exchange.1, s32[1024]{0:T(1024)S(1)} %pad_clamp_fusion), kind=kCustom, calls=%fused_computation | custom fusion | bytes 2097184 | tf_op jit(solution)/shard_map/gather | solution.py:484
  (1 shorter events, 0.0 us)

commit v3 on v2

--- a/solution.py
+++ b/solution.py
@@ -16,13 +16,18 @@
 CHUNK = 4
 NCH = KWR // CHUNK
 PIECE = CHUNK * 2
-HALF = PIECE // 2
+UNITS = NCH * 2
+UNIT = PIECE // 2
+HALF = UNIT // 2
+AHEAD = 2
+MINOR = ROWS // 2 * TILE
 NB = 1024
 NSTEP = NC * TILE // NB
 TOP = 32767.0
 UNROLL = 4
 PHASES = (2, 1, 3, 0)
 MESH = pl.DeviceIdType.MESH
+ORDER = "F0 F1 N0 F2 N1 F3 N2 S0 N3 S1 L0 S2 L1 S3 L2 L3"
 
 
 def encode(v):
@@ -126,58 +131,63 @@
         ib_copy.wait()
         ia_copy.wait()
 
-    def g_copy(q, kind, src, dst_at, n, target):
+    def g_copy(u, kind, src, dst_at, n, target):
         return pltpu.make_async_remote_copy(
             src_ref=src,
-            dst_ref=b_v[q].at[pl.ds(dst_at, n)],
-            send_sem=g_send.at[q, kind],
-            recv_sem=g_recv.at[q, kind],
+            dst_ref=b_v[u // 2].at[pl.ds(dst_at, n)],
+            send_sem=g_send.at[u, kind],
+            recv_sem=g_recv.at[u, kind],
             device_id=target,
             device_id_type=MESH,
         )
 
     up, down, sib = dev_row(1, 0), dev_row(3, 0), dev_row(0, 1)
-    at_own, at_below, at_above, at_far = (at_row(d, 0) * PIECE for d in (0, 3, 1, 2))
-
-    def g_all(q):
-        mine = b_hbm.at[pl.ds(q * PIECE, PIECE)]
-        held = lambda at, n: b_v[q].at[pl.ds(at, n)]
+
+    def g_all(u):
+        at_own, at_below, at_above, at_far = (
+            at_row(d, 0) * PIECE + u % 2 * UNIT for d in (0, 3, 1, 2)
+        )
+        mine = b_hbm.at[pl.ds(u * UNIT, UNIT)]
+        held = lambda at, n: b_v[u // 2].at[pl.ds(at, n)]
         return (
-            g_copy(q, 0, mine, at_own, PIECE, up),
-            g_copy(q, 1, mine, at_own, PIECE, down),
-            g_copy(q, 2, mine, at_own, PIECE, sib),
-            g_copy(q, 3, held(at_below, HALF), at_below, HALF, up),
-            g_copy(q, 4, held(at_above + HALF, HALF), at_above + HALF, HALF, down),
-            g_copy(q, 5, held(at_below, PIECE), at_below, PIECE, sib),
-            g_copy(q, 6, held(at_above, PIECE), at_above, PIECE, sib),
-            g_copy(q, 7, held(at_far, HALF), at_far, HALF, sib),
-            g_copy(q, 8, held(at_far + HALF, HALF), at_far + HALF, HALF, sib),
-        )
-
-    copies = [g_all(q) for q in range(NCH)]
-
-    def first(q):
+            g_copy(u, 0, mine, at_own, UNIT, up),
+            g_copy(u, 1, mine, at_own, UNIT, down),
+            g_copy(u, 2, mine, at_own, UNIT, sib),
+            g_copy(u, 3, held(at_below, HALF), at_below, HALF, up),
+            g_copy(u, 4, held(at_above + HALF, HALF), at_above + HALF, HALF, down),
+            g_copy(u, 5, held(at_below, UNIT), at_below, UNIT, sib),
+            g_copy(u, 6, held(at_above, UNIT), at_above, UNIT, sib),
+            g_copy(u, 7, held(at_far, HALF), at_far, HALF, sib),
+            g_copy(u, 8, held(at_far + HALF, HALF), at_far + HALF, HALF, sib),
+        )
+
+    copies = [g_all(u) for u in range(UNITS)]
+
+    def first(u):
         for kind in (0, 1, 2):
-            copies[q][kind].start()
-
-    def relay(q):
-        copies[q][0].wait_recv()
-        copies[q][3].start()
-        copies[q][5].start()
-        copies[q][1].wait_recv()
-        copies[q][4].start()
-        copies[q][6].start()
-
-    def pass_on(q):
-        copies[q][3].wait_recv()
-        copies[q][7].start()
-        copies[q][4].wait_recv()
-        copies[q][8].start()
+            copies[u][kind].start()
+
+    def relay(u):
+        copies[u][0].wait_recv()
+        copies[u][3].start()
+        copies[u][5].start()
+        copies[u][1].wait_recv()
+        copies[u][4].start()
+        copies[u][6].start()
+        if u + AHEAD < UNITS:
+            first(u + AHEAD)
+
+    def pass_on(u):
+        copies[u][3].wait_recv()
+        copies[u][7].start()
+        copies[u][4].wait_recv()
+        copies[u][8].start()
 
     def arrived(q):
         own[q].wait()
-        for kind in (2, 5, 6, 7, 8):
-            copies[q][kind].wait_recv()
+        for u in (2 * q, 2 * q + 1):
+            for kind in (2, 5, 6, 7, 8):
+                copies[u][kind].wait_recv()
 
     def taken(j):
         total = jnp.int32(0)
@@ -186,44 +196,45 @@
             total = jnp.maximum(total, jnp.where(lax.div(p, ROWS) == row, lax.rem(p, ROWS), 0))
         return total
 
+    def place(d):
+        return d % 2 * MINOR + d // 2 * TILE
+
     def dense_a(q, rows):
         for d in range(ROWS):
             for k in range(CHUNK):
-                ad[d * TILE : (d + 1) * TILE, k * TILE : (k + 1) * TILE] = a_v[
+                ad[place(d) : place(d) + TILE, k * TILE : (k + 1) * TILE] = a_v[
                     ia[rows[d], q * CHUNK + k]
                 ]
 
-    def multiply(q, r0, r1_, hooks=()):
+    def multiply(q, h, n, r0, count):
+        def tile(k, i):
+            col = n * 8 + i if h == 0 else (i // 2 * RING + n) * 2 + i % 2
+            return b_v[q][ib[col, q * CHUNK + k]]
+
+        right = jnp.concatenate(
+            [jnp.concatenate([tile(k, i) for i in range(8)], axis=1) for k in range(CHUNK)], axis=0
+        )
+        cols = pl.ds(pl.multiple_of(n * NB, NB), NB)
+        part = jnp.dot(ad[r0 : r0 + count, :], right, preferred_element_type=jnp.float32)
+        if q == 0:
+            acc[r0 : r0 + count, cols] = part
+        else:
+            acc[r0 : r0 + count, cols] = acc[r0 : r0 + count, cols] + part
+
+    def chunk(q, hooks):
         @pl.loop(0, NSTEP)
         def _(n):
             for step, act in hooks:
                 pl.when(n == step)(act)
-            wide = NB // TILE
-            right = jnp.concatenate(
-                [
-                    jnp.concatenate(
-                        [b_v[q][ib[n * wide + i, q * CHUNK + k]] for i in range(wide)], axis=1
-                    )
-                    for k in range(CHUNK)
-                ],
-                axis=0,
-            )
-            cols = pl.ds(pl.multiple_of(n * NB, NB), NB)
-            part = jnp.dot(ad[r0:r1_, :], right, preferred_element_type=jnp.float32)
-            if q == 0:
-                acc[r0:r1_, cols] = part
-            else:
-                acc[r0:r1_, cols] = acc[r0:r1_, cols] + part
+            for h in range(2):
+                multiply(q, h, n, h * MINOR, MINOR)
 
     def pos(h):
         return (x, z) if h == 0 else (z, x)
 
-    def block(h, f_at, s_at):
-        return f_at * RING + s_at if h == 0 else s_at * RING + f_at
-
-    def held_tile(d, h, f_at, s_at, cc):
-        lanes = pl.ds(pl.multiple_of(block(h, f_at, s_at) * 2 * TILE + cc * TILE, TILE), TILE)
-        return (slice(d * TILE, (d + 1) * TILE), lanes)
+    def held_tile(d, f_at, s_at, cc):
+        lanes = pl.ds(pl.multiple_of((f_at * RING + s_at) * 2 * TILE + cc * TILE, TILE), TILE)
+        return (slice(place(d), place(d) + TILE), lanes)
 
     def m_copy(d, kind, src, dst, target):
         return pltpu.make_async_remote_copy(
@@ -261,7 +272,7 @@
 
             @pl.loop(0, 4, unroll=UNROLL)
             def _(i):
-                v = acc[held_tile(d, h, f2, way * 2 + i // 2, lax.rem(i, 2))]
+                v = acc[held_tile(d, f2, way * 2 + i // 2, lax.rem(i, 2))]
                 coded, scale = encode(v)
                 s1[d, way, i] = coded
                 s1s[d, way, pl.ds(i, 1), :] = scale
@@ -279,14 +290,14 @@
 
             @pl.loop(0, 4, unroll=UNROLL)
             def _(i):
-                v = acc[held_tile(d, h, fd, (1 - way) * 2 + i // 2, lax.rem(i, 2))]
+                v = acc[held_tile(d, fd, (1 - way) * 2 + i // 2, lax.rem(i, 2))]
                 coded, scale = encode(v)
                 s2[d, way, (1 - way) * 4 + i] = coded
                 s2s[d, way, pl.ds((1 - way) * 4 + i, 1), :] = scale
 
             @pl.loop(0, 4, unroll=UNROLL)
             def _(i):
-                v = acc[held_tile(d, h, fd, way * 2 + i // 2, lax.rem(i, 2))]
+                v = acc[held_tile(d, fd, way * 2 + i // 2, lax.rem(i, 2))]
                 v = v + decode(r1[d, way, i], r1s[d, way, pl.ds(i, 1), :])
                 coded, scale = encode(v)
                 s2[d, way, way * 4 + i] = coded
@@ -305,7 +316,7 @@
 
             @pl.loop(0, 2, unroll=2)
             def _(cc):
-                where = held_tile(d, h, f, s_at, cc)
+                where = held_tile(d, f, s_at, cc)
                 i = s_at * 2 + cc
                 v = (
                     acc[where]
@@ -358,66 +369,68 @@
         step(2 * t)
         step(2 * t + 1)
 
-    first(0)
-    first(1)
+    for u in range(AHEAD):
+        first(u)
     tables()
     rows = [taken(at_row(dy, h)) for dy in PHASES for h in range(2)]
     relay(0)
-    first(2)
     relay(1)
-    first(3)
     pass_on(0)
+    relay(2)
+    pass_on(1)
     a_copy.wait()
     arrived(0)
     for q in range(NCH - 1):
         dense_a(q, rows)
-        hooks = []
-        if q + 2 < NCH:
-
-            def onward(q=q):
-                relay(q + 2)
-                if q + 4 < NCH:
-                    first(q + 4)
-
-            hooks.append((NSTEP - 1, onward))
-        else:
-            hooks.append((NSTEP - 2, functools.partial(pass_on, q + 1)))
-        multiply(q, 0, ROWS * TILE, hooks)
-        if q + 2 < NCH:
-            pass_on(q + 1)
+        hooks = [(2, functools.partial(pass_on, 2 * q + 2))]
+        hooks.append((1, functools.partial(relay, 2 * q + 3)))
+        if 2 * q + 4 < UNITS:
+            hooks.append((3, functools.partial(relay, 2 * q + 4)))
+        chunk(q, hooks)
+        pass_on(2 * q + 3)
         arrived(q + 1)
     dense_a(NCH - 1, rows)
 
     def ready(t):
-        multiply(NCH - 1, 2 * t * TILE, 2 * (t + 1) * TILE)
-        both(far_part, t)
-
-    ready(0)
-    ready(1)
-    both(near_part, 0)
-    ready(2)
-    both(near_part, 1)
-    ready(3)
-    both(near_part, 2)
-    both(second, 0)
-    both(near_part, 3)
-    both(second, 1)
-    both(last, 0)
-    both(second, 2)
-    both(last, 1)
-    both(second, 3)
-    both(last, 2)
-    both(last, 3)
-
-    for copy in w_copies:
-        copy.wait_send()
-    for q in range(NCH):
-        for copy in copies[q]:
+        for h in range(2):
+            f, _ = pos(h)
+            multiply(NCH - 1, h, lax.rem(f + 2, RING), place(2 * t + h), TILE)
+            far_part(2 * t + h)
+        for h in range(2):
+            f, _ = pos(h)
+
+            @pl.loop(0, NSTEP - 1)
+            def _(i):
+                multiply(NCH - 1, h, lax.rem(f + 3 + i, RING), place(2 * t + h), TILE)
+
+    def sent():
+        for copy in w_copies:
             copy.wait_send()
-    for d in range(ROWS):
-        for copy in m[d]:
-            copy.wait_send()
-        y_copies[d].wait()
+        for u in range(UNITS):
+            for copy in copies[u]:
+                copy.wait_send()
+
+    def sent_part(t, kinds):
+        for d in (2 * t, 2 * t + 1):
+            for kind in kinds:
+                m[d][kind].wait_send()
+
+    near = functools.partial(both, near_part)
+    across = functools.partial(both, second)
+    finish = functools.partial(both, last)
+
+    steps = {"F": ready, "N": near, "S": across, "L": finish}
+    for word in ORDER.split():
+        t = int(word[1])
+        if word == "S0":
+            sent()
+        if word[0] == "L":
+            sent_part(t, range(8))
+        steps[word[0]](t)
+    for t in range(ROWS // 2):
+        sent_part(t, range(8, 14))
+    for copy in y_copies:
+        copy.wait()
 
 
 def exchange(row_perm, a_cols, b_cols, a_vals, b_vals):
@@ -461,7 +474,7 @@
             pltpu.VMEM((ROWS, 3, 2, *t2), i16),
             pltpu.VMEM((ROWS, 3, 8, TILE), f32),
             pltpu.VMEM((ROWS, 2, *t2), f32),
-            dma((NCH, 9)), dma((NCH, 9)), dma((NCH + 3,)), dma((ROWS,)), dma((ROWS,)),
+            dma((UNITS, 9)), dma((UNITS, 9)), dma((NCH + 3,)), dma((ROWS,)), dma((ROWS,)),
             dma((ROWS, 14)), dma((ROWS, 14)), dma((ROWS,)), dma((ROWS,)),
         ],
         compiler_params=pltpu.CompilerParams(

time: 129 us -> 127 us (0.984)
  Pallas kernels: 126 us -> 123 us
    pallas_call x1, Pallas kernels: 126 us -> 123 us  [exchange(): pl.pallas_call(kernel, out_shape=jax.ShapeDtypeStruct((ROWS, 2, *t2), f32...]
where the time goes in v3:
time: 127 us; the launch traced here: 126 us
  Pallas kernels  123 us (97%)
  local copies, waits for them, and re-layouts  2.81 us (2%)
    pallas_call x1, Pallas kernels, exchange(): pl.pallas_call(kernel, out_shape=jax.ShapeDtypeStruct((ROWS, 2, *t2), f32...  123 us
    gather x1, local copies, waits for them, and re-layouts, on_device(): return got.at[source].get(mode='promise_in_bounds')  2.81 us

profile of v3, /device:TPU:1, one launch (start us, length us, event | category | flops | bytes accessed | tf_op | source)
XLA Modules:
  0.0 126.5 jit_solution(12251523906061030364)
XLA Ops:
  0.0 0.7 compare_select_fusion
  0.7 122.9 %exchange.1 = f32[8,2,128,128]{3,2,1,0:T(8,128)} custom-call(s32[64]{0:T(128)} %perm.1, s32[8,12]{1,0:T(8,128)} %bitcast.6, s32[2,24]{1,0:T(2,128)} %bitcast.7, bf16[96,128,128]{2,1,0:T(8,128)(2,1)} %bitcast.4, bf16[48,128,128]{2,1,0:T(8,128)(2,1)} %bitcast.5), custom_call_target="tpu_custom_call" | custom-call | tf_op jit(solution)/shard_map/exchange/pallas_call | solution.py:441
  123.6 2.8 %gather_fusion = f32[8,2,128,128]{3,2,1,0:T(8,128)} fusion(f32[8,2,128,128]{3,2,1,0:T(8,128)} %exchange.1, s32[1024]{0:T(1024)S(1)} %pad_clamp_fusion), kind=kCustom, calls=%fused_computation | custom fusion | bytes 2097184 | tf_op jit(solution)/shard_map/gather | solution.py:497
  (1 shorter events, 0.0 us)

commit v4 on v3

--- a/solution.py
+++ b/solution.py
@@ -27,7 +27,10 @@
 UNROLL = 4
 PHASES = (2, 1, 3, 0)
 MESH = pl.DeviceIdType.MESH
-ORDER = "F0 F1 N0 F2 N1 F3 N2 S0 N3 S1 L0 S2 L1 S3 L2 L3"
+ORDER = (
+    ("F", 0), ("F", 1), ("N", 0), ("F", 2), ("N", 1), ("F", 3), ("N", 2), ("S", 0),
+    ("N", 3), ("S", 1), ("L", 0), ("S", 2), ("L", 1), ("S", 3), ("L", 2), ("L", 3),
+)
 
 
 def encode(v):
@@ -420,13 +423,12 @@
     finish = functools.partial(both, last)
 
     steps = {"F": ready, "N": near, "S": across, "L": finish}
-    for word in ORDER.split():
-        t = int(word[1])
-        if word == "S0":
+    for step, t in ORDER:
+        if step == "S" and t == 0:
             sent()
-        if word[0] == "L":
+        if step == "L":
             sent_part(t, range(8))
-        steps[word[0]](t)
+        steps[step](t)
     for t in range(ROWS // 2):
         sent_part(t, range(8, 14))
     for copy in y_copies:

time: 127 us -> 127 us (level)
  no operation moved by 1% of the time
where the time goes in v4:
time: 127 us; the launch traced here: 126 us
  Pallas kernels  123 us (97%)
  local copies, waits for them, and re-layouts  2.81 us (2%)
    pallas_call x1, Pallas kernels, exchange(): pl.pallas_call(kernel, out_shape=jax.ShapeDtypeStruct((ROWS, 2, *t2), f32...  123 us
    gather x1, local copies, waits for them, and re-layouts, on_device(): return got.at[source].get(mode='promise_in_bounds')  2.81 us

profile of v4, /device:TPU:1, one launch (start us, length us, event | category | flops | bytes accessed | tf_op | source)
XLA Modules:
  0.0 126.5 jit_solution(12251523906061030364)
XLA Ops:
  0.0 0.7 compare_select_fusion
  0.7 122.9 %exchange.1 = f32[8,2,128,128]{3,2,1,0:T(8,128)} custom-call(s32[64]{0:T(128)} %perm.1, s32[8,12]{1,0:T(8,128)} %bitcast.6, s32[2,24]{1,0:T(2,128)} %bitcast.7, bf16[96,128,128]{2,1,0:T(8,128)(2,1)} %bitcast.4, bf16[48,128,128]{2,1,0:T(8,128)(2,1)} %bitcast.5), custom_call_target="tpu_custom_call" | custom-call | tf_op jit(solution)/shard_map/exchange/pallas_call | solution.py:443
  123.6 2.8 %gather_fusion = f32[8,2,128,128]{3,2,1,0:T(8,128)} fusion(f32[8,2,128,128]{3,2,1,0:T(8,128)} %exchange.1, s32[1024]{0:T(1024)S(1)} %pad_clamp_fusion), kind=kCustom, calls=%fused_computation | custom fusion | bytes 2097184 | tf_op jit(solution)/shard_map/gather | solution.py:499
  (1 shorter events, 0.0 us)

commit v5 on v4

--- a/solution.py
+++ b/solution.py
@@ -25,7 +25,7 @@
 NSTEP = NC * TILE // NB
 TOP = 32767.0
 UNROLL = 4
-PHASES = (2, 1, 3, 0)
+DEST = ((2, 0), (2, 1), (1, 0), (3, 0), (1, 1), (3, 1), (0, 0), (0, 1))
 MESH = pl.DeviceIdType.MESH
 ORDER = (
     ("F", 0), ("F", 1), ("N", 0), ("F", 2), ("N", 1), ("F", 3), ("N", 2), ("S", 0),
@@ -338,22 +338,20 @@
                 m[d][7 + 2 * ds].start()
 
     y_copies = []
-    for t, dy in enumerate(PHASES):
-        for h in range(2):
-            d = 2 * t + h
-            if dy or h:
-                y_copies.append(
-                    pltpu.make_async_remote_copy(
-                        src_ref=fin.at[d],
-                        dst_ref=out.at[row],
-                        send_sem=y_send.at[d],
-                        recv_sem=y_recv.at[d],
-                        device_id=dev_row(dy, h),
-                        device_id_type=MESH,
-                    )
+    for d, (dy, dc) in enumerate(DEST):
+        if dy or dc:
+            y_copies.append(
+                pltpu.make_async_remote_copy(
+                    src_ref=fin.at[d],
+                    dst_ref=out.at[row],
+                    send_sem=y_send.at[d],
+                    recv_sem=y_recv.at[d],
+                    device_id=dev_row(dy, dc),
+                    device_id_type=MESH,
                 )
-            else:
-                y_copies.append(pltpu.make_async_copy(fin.at[d], out.at[row], y_send.at[d]))
+            )
+        else:
+            y_copies.append(pltpu.make_async_copy(fin.at[d], out.at[row], y_send.at[d]))
 
     def last(d):
         for kind in range(8, 14):
@@ -375,7 +373,7 @@
     for u in range(AHEAD):
         first(u)
     tables()
-    rows = [taken(at_row(dy, h)) for dy in PHASES for h in range(2)]
+    rows = [taken(at_row(dy, dc)) for dy, dc in DEST]
     relay(0)
     relay(1)
     pass_on(0)
@@ -424,7 +422,7 @@
 
     steps = {"F": ready, "N": near, "S": across, "L": finish}
     for step, t in ORDER:
-        if step == "S" and t == 0:
+        if step == "L" and t == 0:
             sent()
         if step == "L":
             sent_part(t, range(8))

time: 127 us -> 126 us (level)
  no operation moved by 1% of the time
where the time goes in v5:
time: 126 us
  Pallas kernels  122 us (97%)
  local copies, waits for them, and re-layouts  2.81 us (2%)
    pallas_call x1, Pallas kernels, exchange(): pl.pallas_call(kernel, out_shape=jax.ShapeDtypeStruct((ROWS, 2, *t2), f32...  122 us
    gather x1, local copies, waits for them, and re-layouts, on_device(): return got.at[source].get(mode='promise_in_bounds')  2.81 us

profile of v5, /device:TPU:1, one launch (start us, length us, event | category | flops | bytes accessed | tf_op | source)
XLA Modules:
  0.0 125.6 jit_solution(11562278720783057897)
XLA Ops:
  0.0 0.7 compare_select_fusion
  0.7 122.1 %exchange.1 = f32[8,2,128,128]{3,2,1,0:T(8,128)} custom-call(s32[64]{0:T(128)} %perm.1, s32[8,12]{1,0:T(8,128)} %bitcast.6, s32[2,24]{1,0:T(2,128)} %bitcast.7, bf16[96,128,128]{2,1,0:T(8,128)(2,1)} %bitcast.4, bf16[48,128,128]{2,1,0:T(8,128)(2,1)} %bitcast.5), custom_call_target="tpu_custom_call" | custom-call | tf_op jit(solution)/shard_map/exchange/pallas_call | solution.py:441
  122.8 2.8 %gather_fusion = f32[8,2,128,128]{3,2,1,0:T(8,128)} fusion(f32[8,2,128,128]{3,2,1,0:T(8,128)} %exchange.1, s32[1024]{0:T(1024)S(1)} %pad_clamp_fusion), kind=kCustom, calls=%fused_computation | custom fusion | bytes 2097184 | tf_op jit(solution)/shard_map/gather | solution.py:497
  (1 shorter events, 0.0 us)

commit v6 on v5

--- a/solution.py
+++ b/solution.py
@@ -380,17 +380,17 @@
     relay(2)
     pass_on(1)
     a_copy.wait()
+    dense_a(0, rows)
     arrived(0)
     for q in range(NCH - 1):
-        dense_a(q, rows)
         hooks = [(2, functools.partial(pass_on, 2 * q + 2))]
         hooks.append((1, functools.partial(relay, 2 * q + 3)))
         if 2 * q + 4 < UNITS:
             hooks.append((3, functools.partial(relay, 2 * q + 4)))
         chunk(q, hooks)
+        dense_a(q + 1, rows)
         pass_on(2 * q + 3)
         arrived(q + 1)
-    dense_a(NCH - 1, rows)
 
     def ready(t):
         for h in range(2):

time: 126 us -> 126 us (level)
  no operation moved by 1% of the time
where the time goes in v6:
time: 126 us
  Pallas kernels  122 us (97%)
  local copies, waits for them, and re-layouts  2.81 us (2%)
    pallas_call x1, Pallas kernels, exchange(): pl.pallas_call(kernel, out_shape=jax.ShapeDtypeStruct((ROWS, 2, *t2), f32...  122 us
    gather x1, local copies, waits for them, and re-layouts, on_device(): return got.at[source].get(mode='promise_in_bounds')  2.81 us

profile of v6, /device:TPU:1, one launch (start us, length us, event | category | flops | bytes accessed | tf_op | source)
XLA Modules:
  0.0 125.7 jit_solution(14967624586328913220)
XLA Ops:
  0.0 0.7 compare_select_fusion
  0.7 122.1 %exchange.1 = f32[8,2,128,128]{3,2,1,0:T(8,128)} custom-call(s32[64]{0:T(128)} %perm.1, s32[8,12]{1,0:T(8,128)} %bitcast.6, s32[2,24]{1,0:T(2,128)} %bitcast.7, bf16[96,128,128]{2,1,0:T(8,128)(2,1)} %bitcast.4, bf16[48,128,128]{2,1,0:T(8,128)(2,1)} %bitcast.5), custom_call_target="tpu_custom_call" | custom-call | tf_op jit(solution)/shard_map/exchange/pallas_call | solution.py:441
  122.9 2.8 %gather_fusion = f32[8,2,128,128]{3,2,1,0:T(8,128)} fusion(f32[8,2,128,128]{3,2,1,0:T(8,128)} %exchange.1, s32[1024]{0:T(1024)S(1)} %pad_clamp_fusion), kind=kCustom, calls=%fused_computation | custom fusion | bytes 2097184 | tf_op jit(solution)/shard_map/gather | solution.py:497
  (1 shorter events, 0.0 us)

commit v7 on v5

--- a/solution.py
+++ b/solution.py
@@ -424,11 +424,9 @@
     for step, t in ORDER:
         if step == "L" and t == 0:
             sent()
-        if step == "L":
-            sent_part(t, range(8))
         steps[step](t)
     for t in range(ROWS // 2):
-        sent_part(t, range(8, 14))
+        sent_part(t, range(14))
     for copy in y_copies:
         copy.wait()
 

time: 126 us -> 126 us (level)
  no operation moved by 1% of the time
where the time goes in v7:
time: 126 us
  Pallas kernels  122 us (97%)
  local copies, waits for them, and re-layouts  2.81 us (2%)
    pallas_call x1, Pallas kernels, exchange(): pl.pallas_call(kernel, out_shape=jax.ShapeDtypeStruct((ROWS, 2, *t2), f32...  122 us
    gather x1, local copies, waits for them, and re-layouts, on_device(): return got.at[source].get(mode='promise_in_bounds')  2.81 us

profile of v7, /device:TPU:1, one launch (start us, length us, event | category | flops | bytes accessed | tf_op | source)
XLA Modules:
  0.0 125.6 jit_solution(5414902910950867252)
XLA Ops:
  0.0 0.7 compare_select_fusion
  0.7 122.1 %exchange.1 = f32[8,2,128,128]{3,2,1,0:T(8,128)} custom-call(s32[64]{0:T(128)} %perm.1, s32[8,12]{1,0:T(8,128)} %bitcast.6, s32[2,24]{1,0:T(2,128)} %bitcast.7, bf16[96,128,128]{2,1,0:T(8,128)(2,1)} %bitcast.4, bf16[48,128,128]{2,1,0:T(8,128)(2,1)} %bitcast.5), custom_call_target="tpu_custom_call" | custom-call | tf_op jit(solution)/shard_map/exchange/pallas_call | solution.py:439
  122.8 2.8 %gather_fusion = f32[8,2,128,128]{3,2,1,0:T(8,128)} fusion(f32[8,2,128,128]{3,2,1,0:T(8,128)} %exchange.1, s32[1024]{0:T(1024)S(1)} %pad_clamp_fusion), kind=kCustom, calls=%fused_computation | custom fusion | bytes 2097184 | tf_op jit(solution)/shard_map/gather | solution.py:495
  (1 shorter events, 0.0 us)
